TPU v7x, 32 devices: a whole 2x2x4 slice. The times are simulated.
32 devices in a mesh: row: 4 (over y, core), col: 8 (over z, x).
Axes of the slice: x: 2, y: 2, z: 4, core: 2. Of those that a mesh axis runs over, the one named last changes fastest.
Arguments:
- row_gen: bfloat16 [64, 1024, 256], P(('row', 'col')), may hold values from -6 to 6
- row_upd: bfloat16 [64, 1024, 256], P(('row', 'col')), may hold values from -6 to 6
- col_gen: bfloat16 [64, 1024, 256], P('row', 'col'), may hold values from -6 to 6
- col_upd: bfloat16 [64, 1024, 256], P('row', 'col'), may hold values from -6 to 6
- leaf_rank: int32 [64], P(('row', 'col')), may hold values from 32 to 256, as said below
- leaf_trunc: int32 [64], P(('row', 'col')), may hold values from 128 to 512
- node_trunc: int32 [4, 14], replicated, may hold values from 128 to 384, as said below
- coupling: float32 [2048, 512], P(('row', 'col')), may hold values from -6 to 6
Outputs:
- recompressed: float32 [2048, 512], P(('row', 'col'))
Inputs may be any that keep to these rules, and one draw needn't show every extreme that they name: `leaf_rank`: the first leaf of every device (leaf indices that are multiples of 2) has rank 256. `node_trunc`: column 0 (the first height-0 node of each top node) is 384 in every row.
All inputs are finite; a program needn't handle non-finite values.
Results may differ from a plain program's by a relative error of at most 0.0003.
Values may be sent and summed in bfloat16 or wider, within the bound.
A program may use at most 128 MiB of HBM per device.

v0:
```python
import jax
import jax.numpy as jnp
from jax import lax
from jax.sharding import PartitionSpec as P

HIGH = lax.Precision.HIGHEST
OFFSETS = (0, 8, 12)


def partner(block, axis, distance):
    count = lax.axis_size(axis)
    route = []
    for low in range(count):
        high = low | 1 << distance
        if high != low and high < count:
            route += [(low, high), (high, low)]
    return lax.ppermute(block, axis, route)


def both_factors(generators, updates, ranks, truncs):
    leaf_count = ranks.shape[0] // 2
    width_gen = generators.shape[2]
    col_ids = lax.broadcasted_iota(jnp.int32, (1, 1, width_gen), 2)
    keep_cols = (col_ids < ranks[:, None, None]).astype(generators.dtype)
    stacked = jnp.concatenate([generators * keep_cols, updates], axis=2)
    gram_matrix = jnp.einsum("nlk,nlm->nkm", stacked, stacked, preferred_element_type=jnp.float32)
    width_all = gram_matrix.shape[1]
    gram_matrix = gram_matrix + jnp.eye(width_all, dtype=jnp.float32)
    factor = jnp.swapaxes(jnp.linalg.cholesky(gram_matrix), 1, 2)
    row_ids = lax.broadcasted_iota(jnp.int32, (1, width_all, 1), 1)
    kept_rows = factor * (row_ids < truncs[:, None, None]).astype(jnp.float32)
    kept_rows = kept_rows.reshape(2, leaf_count * width_all, width_all)
    node_gram = jnp.einsum("srk,srm->skm", kept_rows, kept_rows, precision=HIGH) + jnp.eye(
        width_all, dtype=jnp.float32
    )
    return jnp.swapaxes(jnp.linalg.cholesky(node_gram), 1, 2)


def truncate(factors, keep_rank):
    row_ids = lax.broadcasted_iota(jnp.int32, (1, factors.shape[1], 1), 1)
    return factors * (row_ids < keep_rank).astype(jnp.float32)


def merge_pair(own_rows, other_rows):
    width_all = own_rows.shape[2]
    gram_matrix = jnp.einsum("srk,srm->skm", own_rows, own_rows, precision=HIGH)
    gram_matrix = gram_matrix + jnp.einsum("srk,srm->skm", other_rows, other_rows, precision=HIGH)
    gram_matrix = gram_matrix + jnp.eye(width_all, dtype=jnp.float32)
    return jnp.swapaxes(jnp.linalg.cholesky(gram_matrix), 1, 2)


def body(row_gen, row_upd, col_gen, col_upd, leaf_rank, leaf_trunc, node_trunc, coupling):
    col_gen_full, col_upd_full = (
        lax.all_to_all(col_gen, "col", split_axis=0, concat_axis=1, tiled=True),
        lax.all_to_all(col_upd, "col", split_axis=0, concat_axis=1, tiled=True),
    )
    generators = jnp.concatenate([row_gen, col_gen_full], 0)
    updates = jnp.concatenate([row_upd, col_upd_full], 0)
    ranks = jnp.concatenate([leaf_rank, leaf_rank], 0)
    truncs = jnp.concatenate([leaf_trunc, leaf_trunc], 0)
    factors = both_factors(generators, updates, ranks, truncs)
    row_pos = lax.axis_index("row")
    col_pos = lax.axis_index("col")
    groups = lax.axis_size("col") // 8
    top_node = row_pos * groups + col_pos // 8
    member = col_pos % 8
    width_all = factors.shape[1]
    for height in range(3):
        keep_rank = node_trunc[top_node, OFFSETS[height] + (member >> height)]
        kept = truncate(factors, keep_rank)
        row_other, col_other = partner((kept[0], kept[1]), "col", height)
        factors = merge_pair(kept, jnp.stack([row_other, col_other], 0))
    row_factor = factors[0]
    col_factor = factors[1]
    partner_col = partner(col_factor, "row", 0)
    share_rows = width_all // 8
    my_rows = lax.dynamic_slice_in_dim(row_factor, member * share_rows, share_rows, 0)
    group_start = col_pos // 8 * width_all
    piece_rows = lax.all_gather(coupling, "col", axis=0, tiled=True)
    row_count = piece_rows.shape[0]
    positions = lax.broadcasted_iota(jnp.int32, (row_count,), 0) - group_start
    inside = (positions >= 0) & (positions < width_all)
    picked = jnp.take(my_rows, jnp.clip(positions, 0, width_all - 1), axis=1)
    picked = picked * inside.astype(jnp.float32)[None, :]
    projected = jnp.dot(picked, piece_rows, precision=HIGH)
    result = jnp.dot(projected, partner_col.T, precision=HIGH)
    return result / (8 * row_gen.shape[0] * row_gen.shape[1])


def solution(mesh):
    return jax.shard_map(
        body,
        mesh=mesh,
        in_specs=(
            P(("row", "col"), None, None),
            P(("row", "col"), None, None),
            P("row", "col", None),
            P("row", "col", None),
            P(("row", "col")),
            P(("row", "col")),
            P(),
            P(("row", "col"), None),
        ),
        out_specs=P(("row", "col"), None),
        check_vma=False,
    )
```

profile of v0, /device:TPU:1, one launch (start us, length us, event | category | flops | bytes accessed | tf_op | source)
XLA Modules:
  0.0 1381.0 jit_solution(1498919530769658933)
XLA Ops:
  6.5 31.4 %all_to_all.36 = bf16[16,128,256]{2,1,0:T(8,128)(2,1)} all-to-all(bf16[16,128,256]{2,1,0:T(8,128)(2,1)} %param.11), channel_id=1, replica_groups=mesh['row'=4,'col'=8] {'col'}, dimensions={0} | all-to-all | bytes 2097152 | tf_op jit(solution)/shard_map/all_to_all | solution.py:54
  86.0 46.9 %custom-call.55 = f32[4,128,128]{2,1,0:T(8,128)S(1)} custom-call(f32[4,128,128]{2,1,0:T(8,128)S(1)} %cholesky.1016), custom_call_target="Cholesky" | custom-call | tf_op jit(solution)/shard_map/jit(cholesky)/cholesky | solution.py:29
  132.9 39.3 %custom-call.56 = f32[4,1,128,128]{2,3,1,0:T(8,128)S(1)} custom-call(f32[4,1,128,128]{3,2,1,0:T(8,128)S(1)} %select_bitcast_fusion.3), custom_call_target="InvertDiagBlocksLowerTriangular" | custom-call | tf_op jit(solution)/shard_map/jit(cholesky)/cholesky | solution.py:29
  180.7 48.1 %custom-call.57 = f32[4,128,128]{2,1,0:T(8,128)S(1)} custom-call(f32[4,128,128]{2,1,0:T(8,128)} %cholesky.1020), custom_call_target="Cholesky" | custom-call | tf_op jit(solution)/shard_map/jit(cholesky)/cholesky | solution.py:29
  230.6 39.3 %custom-call.58 = f32[4,1,128,128]{2,3,1,0:T(8,128)S(1)} custom-call(f32[4,1,128,128]{3,2,1,0:T(8,128)S(1)} %get-tuple-element.37), custom_call_target="InvertDiagBlocksLowerTriangular" | custom-call | tf_op jit(solution)/shard_map/jit(cholesky)/cholesky | solution.py:29
  274.0 46.9 %custom-call.59 = f32[4,128,128]{2,1,0:T(8,128)S(1)} custom-call(f32[4,128,128]{2,1,0:T(8,128)S(1)} %cholesky.1025), custom_call_target="Cholesky" | custom-call | tf_op jit(solution)/shard_map/jit(cholesky)/cholesky | solution.py:29
  321.7 39.5 %custom-call.60 = f32[4,1,128,128]{2,3,1,0:T(8,128)S(1)} custom-call(f32[4,1,128,128]{3,2,1,0:T(8,128)S(1)} %get-tuple-element.35), custom_call_target="InvertDiagBlocksLowerTriangular" | custom-call | tf_op jit(solution)/shard_map/jit(cholesky)/cholesky | solution.py:29
  364.9 46.9 %custom-call.61 = f32[4,128,128]{2,1,0:T(8,128)S(1)} custom-call(f32[4,128,128]{2,1,0:T(8,128)S(1)} %convolution_subtract_fusion.10), custom_call_target="Cholesky" | custom-call | tf_op jit(solution)/shard_map/jit(cholesky)/cholesky | solution.py:29
  439.0 23.5 %custom-call.83 = f32[2,128,128]{2,1,0:T(8,128)S(1)} custom-call(f32[2,128,128]{2,1,0:T(8,128)S(1)} %cholesky.1029), custom_call_target="Cholesky" | custom-call | tf_op jit(solution)/shard_map/jit(cholesky)/cholesky | solution.py:36
  489.0 25.3 %custom-call.85 = f32[2,128,128]{2,1,0:T(8,128)} custom-call(f32[2,128,128]{2,1,0:T(8,128)} %cholesky.1033), custom_call_target="Cholesky" | custom-call | tf_op jit(solution)/shard_map/jit(cholesky)/cholesky | solution.py:36
  541.3 24.9 %custom-call.87 = f32[2,128,128]{2,1,0:T(8,128)} custom-call(f32[2,128,128]{2,1,0:T(8,128)} %cholesky.1038), custom_call_target="Cholesky" | custom-call | tf_op jit(solution)/shard_map/jit(cholesky)/cholesky | solution.py:36
  592.4 25.1 %custom-call.89 = f32[2,128,128]{2,1,0:T(8,128)} custom-call(f32[2,128,128]{2,1,0:T(8,128)} %convolution_subtract_fusion.14), custom_call_target="Cholesky" | custom-call | tf_op jit(solution)/shard_map/jit(cholesky)/cholesky | solution.py:36
  675.2 23.9 %custom-call.90 = f32[2,128,128]{2,1,0:T(8,128)S(1)} custom-call(f32[2,128,128]{2,1,0:T(8,128)S(1)} %cholesky.1042), custom_call_target="Cholesky" | custom-call | tf_op jit(solution)/shard_map/jit(cholesky)/cholesky | solution.py:49
  725.6 24.9 %custom-call.92 = f32[2,128,128]{2,1,0:T(8,128)} custom-call(f32[2,128,128]{2,1,0:T(8,128)} %cholesky.1046), custom_call_target="Cholesky" | custom-call | tf_op jit(solution)/shard_map/jit(cholesky)/cholesky | solution.py:49
  777.6 24.9 %custom-call.94 = f32[2,128,128]{2,1,0:T(8,128)} custom-call(f32[2,128,128]{2,1,0:T(8,128)} %cholesky.1051), custom_call_target="Cholesky" | custom-call | tf_op jit(solution)/shard_map/jit(cholesky)/cholesky | solution.py:49
  828.6 25.1 %custom-call.96 = f32[2,128,128]{2,1,0:T(8,128)} custom-call(f32[2,128,128]{2,1,0:T(8,128)} %convolution_subtract_fusion.13), custom_call_target="Cholesky" | custom-call | tf_op jit(solution)/shard_map/jit(cholesky)/cholesky | solution.py:49
  909.7 23.9 %custom-call.97 = f32[2,128,128]{2,1,0:T(8,128)S(1)} custom-call(f32[2,128,128]{2,1,0:T(8,128)S(1)} %cholesky.1055), custom_call_target="Cholesky" | custom-call | tf_op jit(solution)/shard_map/jit(cholesky)/cholesky | solution.py:49
  960.0 24.9 %custom-call.99 = f32[2,128,128]{2,1,0:T(8,128)} custom-call(f32[2,128,128]{2,1,0:T(8,128)} %cholesky.1059), custom_call_target="Cholesky" | custom-call | tf_op jit(solution)/shard_map/jit(cholesky)/cholesky | solution.py:49
  1012.1 24.9 %custom-call.101 = f32[2,128,128]{2,1,0:T(8,128)} custom-call(f32[2,128,128]{2,1,0:T(8,128)} %cholesky.1064), custom_call_target="Cholesky" | custom-call | tf_op jit(solution)/shard_map/jit(cholesky)/cholesky | solution.py:49
  1063.1 25.1 %custom-call.103 = f32[2,128,128]{2,1,0:T(8,128)} custom-call(f32[2,128,128]{2,1,0:T(8,128)} %convolution_subtract_fusion.12), custom_call_target="Cholesky" | custom-call | tf_op jit(solution)/shard_map/jit(cholesky)/cholesky | solution.py:49
  1100.9 67.8 %collective-permute-done.4 = f32[512,512]{0,1:T(8,128)} collective-permute-done((f32[512,512]{0,1:T(8,128)}, f32[512,512]{0,1:T(8,128)}, u32[]{:S(2)}, u32[]{:S(2)}) %collective-permute-start.4) | collective-permute-done | bytes 1048608 | tf_op jit(solution)/shard_map/ppermute | solution.py:17
  1202.5 23.9 %custom-call.104 = f32[2,128,128]{2,1,0:T(8,128)S(1)} custom-call(f32[2,128,128]{2,1,0:T(8,128)S(1)} %cholesky.1068), custom_call_target="Cholesky" | custom-call | tf_op jit(solution)/shard_map/jit(cholesky)/cholesky | solution.py:49
  1250.7 23.5 %custom-call.106 = f32[2,128,128]{2,1,0:T(8,128)S(1)} custom-call(f32[2,128,128]{2,1,0:T(8,128)S(1)} %cholesky.1072), custom_call_target="Cholesky" | custom-call | tf_op jit(solution)/shard_map/jit(cholesky)/cholesky | solution.py:49
  1342.0 23.7 %custom-call.110 = f32[2,128,128]{2,1,0:T(8,128)S(1)} custom-call(f32[2,128,128]{2,1,0:T(8,128)S(1)} %convolution_subtract_fusion.11), custom_call_target="Cholesky" | custom-call | tf_op jit(solution)/shard_map/jit(cholesky)/cholesky | solution.py:49
  (230 shorter events, 593.2 us)
Async XLA Ops:
  37.9 28.4 %all-to-all-start.1 = ((bf16[16,128,256]{2,1,0:T(8,128)(2,1)}), bf16[16,128,256]{2,1,0:T(8,128)(2,1)}, u32[]{:S(2)}, u32[]{:S(2)}) async-start(bf16[16,128,256]{2,1,0:T(8,128)(2,1)} %param.12), calls=%async_computation.1 | async-start | bytes 2097152 | tf_op jit(solution)/shard_map/all_to_all | solution.py:55
  42.2 1.4 copy-start.24
  42.2 1328.2 %all-gather.2.cloned.1.call-start = ((), (), s32[]{:S(2)}) async-start(), calls=%async_computation.2 | async-start | bytes 1179648 | tf_op jit(solution)/shard_map/all_gather | solution.py:79
  44.9 366.9 %copy-start.16 = (pred[128,128]{1,0:T(8,128)(4,1)}, pred[128,128]{1,0:T(8,128)(4,1)S(1)}, u32[]{:S(2)}) copy-start(pred[128,128]{1,0:T(8,128)(4,1)S(1)} %iota_compare_fusion.3) | copy-start | bytes 49156
  66.3 1.5 copy-start.5
  66.3 1.9 copy-start.15
  84.0 1.9 copy-start
  177.4 2.5 copy-start.6
  180.7 89.2 %copy-start.7 = (f32[4,384,128]{2,1,0:T(8,128)S(1)}, f32[4,384,128]{2,1,0:T(8,128)}, u32[]{:S(2)}) copy-start(f32[4,384,128]{2,1,0:T(8,128)} %copy-done.6) | copy-start | bytes 2359300
  437.7 1.4 copy-start.2
  620.1 3.9 copy-start.18
  620.3 23.5 %collective-permute-start = (f32[512,512]{0,1:T(8,128)S(1)}, f32[512,512]{0,1:T(8,128)S(1)}, u32[]{:S(2)}, u32[]{:S(2)}) collective-permute-start(f32[512,512]{0,1:T(8,128)S(1)} %get-tuple-element.32), channel_id=1, source_target_pairs={{0,1},{1,0},{2,3},{3,2},{4,5},{5,4},{6,7},{7,6},{8,9},{9,8},{10,11... | collective-permute-start | bytes 3145736 | tf_op jit(solution)/shard_map/ppermute | solution.py:17
  622.7 43.7 %collective-permute-start.1 = (f32[512,512]{0,1:T(8,128)S(1)}, f32[512,512]{0,1:T(8,128)S(1)}, u32[]{:S(2)}, u32[]{:S(2)}) collective-permute-start(f32[512,512]{0,1:T(8,128)S(1)} %get-tuple-element.33), channel_id=1, source_target_pairs={{0,1},{1,0},{2,3},{3,2},{4,5},{5,4},{6,7},{7,6},{8,9},{9,8},{10,11... | collective-permute-start | bytes 3145736 | tf_op jit(solution)/shard_map/ppermute | solution.py:17
  673.9 1.4 copy-start.3
  856.3 2.9 copy-start.20
  856.5 21.8 %collective-permute-start.2 = (f32[512,512]{0,1:T(8,128)S(1)}, f32[512,512]{0,1:T(8,128)S(1)}, u32[]{:S(2)}, u32[]{:S(2)}) collective-permute-start(f32[512,512]{0,1:T(8,128)S(1)} %get-tuple-element.30), channel_id=1, source_target_pairs={{0,2},{2,0},{1,3},{3,1},{4,6},{6,4},{5,7},{7,5},{8,10},{10,8},{9,1... | collective-permute-start | bytes 3145736 | tf_op jit(solution)/shard_map/ppermute | solution.py:17
  856.7 44.1 %collective-permute-start.3 = (f32[512,512]{0,1:T(8,128)S(1)}, f32[512,512]{0,1:T(8,128)S(1)}, u32[]{:S(2)}, u32[]{:S(2)}) collective-permute-start(f32[512,512]{0,1:T(8,128)S(1)} %get-tuple-element.31), channel_id=1, source_target_pairs={{0,2},{2,0},{1,3},{3,1},{4,6},{6,4},{5,7},{7,5},{8,10},{10,8},{9,1... | collective-permute-start | bytes 3145736 | tf_op jit(solution)/shard_map/ppermute | solution.py:17
  908.3 1.4 copy-start.4
  1090.8 5.9 copy-start.19
  1092.3 76.4 %collective-permute-start.4 = (f32[512,512]{0,1:T(8,128)}, f32[512,512]{0,1:T(8,128)}, u32[]{:S(2)}, u32[]{:S(2)}) collective-permute-start(f32[512,512]{0,1:T(8,128)} %get-tuple-element.28), channel_id=1, source_target_pairs={{0,4},{4,0},{1,5},{5,1},{2,6},{6,2},{3,7},{7,3},{8,12},{12,8},{9,1... | collective-permute-start | bytes 3145736 | tf_op jit(solution)/shard_map/ppermute | solution.py:17
  1096.6 94.6 %collective-permute-start.5 = (f32[512,512]{0,1:T(8,128)}, f32[512,512]{0,1:T(8,128)}, u32[]{:S(2)}, u32[]{:S(2)}) collective-permute-start(f32[512,512]{0,1:T(8,128)} %get-tuple-element.29), channel_id=1, source_target_pairs={{0,4},{4,0},{1,5},{5,1},{2,6},{6,2},{3,7},{7,3},{8,12},{12,8},{9,1... | collective-permute-start | bytes 3145736 | tf_op jit(solution)/shard_map/ppermute | solution.py:17
  1201.1 1.4 copy-start.1
  1274.2 91.5 %copy-start.17 = (pred[128,128]{1,0:T(8,128)(4,1)S(1)}, pred[128,128]{1,0:T(8,128)(4,1)}, u32[]{:S(2)}) copy-start(pred[128,128]{1,0:T(8,128)(4,1)} %copy-done.16) | copy-start | bytes 49156
  1367.8 4.7 collective-permute-start.6
  (10 other events, 8.5 us)
Sparse Core Ops, SparseCore 0:
  1096.8 116.9 all-gather.1
where the time goes:
time: 1390 us; the launch traced here: 1380 us
  other arithmetic  993 us (71%)
  waiting for transfers between devices  184 us (13%)
  matrix products  93.4 us (7%)
  local copies, waits for them, and re-layouts  50.8 us (4%)
  blocking collectives  31.4 us (2%)
  between operations  14.6 us (1%)
  starting transfers between devices  13.9 us (1%)
    another operation x49, other arithmetic, merge_pair(): return jnp.swapaxes(jnp.linalg.cholesky(gram_matrix), 1, 2)  489 us
    another operation x15, other arithmetic, both_factors(): factor = jnp.swapaxes(jnp.linalg.cholesky(gram_matrix), 1, 2)  310 us
    another operation x16, other arithmetic, both_factors(): return jnp.swapaxes(jnp.linalg.cholesky(node_gram), 1, 2)  168 us
    ppermute x7, waiting for transfers between devices, partner(): return lax.ppermute(block, axis, route)  166 us
    all_to_all x1, blocking collectives, body(): lax.all_to_all(col_gen, 'col', split_axis=0, concat_axis=1, tiled=True)  31.4 us
  transfers between devices with their start and end apart: 9, of which 7 were waited for; matrix products, arithmetic and copies ran while one was open for 14% of the time, Pallas kernels for 0%

commit v1 on v0

--- a/solution.py
+++ b/solution.py
@@ -5,6 +5,19 @@
 
 HIGH = lax.Precision.HIGHEST
 OFFSETS = (0, 8, 12)
+
+
+def close_fields(u_in, array_dim, local_block):
+    frame_out, e_next = (u_in.shape[:array_dim], u_in.shape[array_dim + 1 :])
+    t1 = jnp.moveaxis(u_in.reshape(*frame_out, local_block, -1, *e_next), array_dim, 0)
+    return t1
+
+
+def see_group(a0, at_axis):
+    after = list(a0.shape[1:])
+    after[at_axis] *= a0.shape[0]
+    arr_out = jnp.moveaxis(a0, 0, at_axis).reshape(after)
+    return arr_out
 
 
 def partner(block, axis, distance):
@@ -50,8 +63,22 @@
 
 
 def body(row_gen, row_upd, col_gen, col_upd, leaf_rank, leaf_trunc, node_trunc, coupling):
+
+    def zone_point(page, row_axis, chunk, u):
+        row_out, r2 = (lax.axis_size(row_axis), lax.axis_index(row_axis))
+        main = close_fields(page, chunk, row_out)
+        buffers = [main[r2]]
+        for k in [*range(1, row_out)]:
+            step_out = main[r2 ^ k]
+            buffers.append(
+                lax.ppermute(step_out, row_axis, [(at, at ^ k) for at in range(row_out)])
+            )
+        main = jnp.stack(buffers, axis=0)[r2 ^ jnp.arange(row_out)]
+        z2 = see_group(main, u)
+        return z2
+
     col_gen_full, col_upd_full = (
-        lax.all_to_all(col_gen, "col", split_axis=0, concat_axis=1, tiled=True),
+        zone_point(col_gen, "col", 0, 1),
         lax.all_to_all(col_upd, "col", split_axis=0, concat_axis=1, tiled=True),
     )
     generators = jnp.concatenate([row_gen, col_gen_full], 0)

time: 1390 us -> 1390 us (level)
  blocking collectives: 31.4 us -> 0 us
  starting transfers between devices: 13.9 us -> 34.7 us
    all_to_all x1 -> x0, blocking collectives: 31.4 us -> none  [body(): lax.all_to_all(col_gen, 'col', split_axis=0, concat_axis=1, tiled=True)]
    all_to_all x1, waiting for transfers between devices: 18.7 us -> 1.05 us  [body(): lax.all_to_all(col_upd, 'col', split_axis=0, concat_axis=1, tiled=True)]
    another operation x15 -> x17, other arithmetic: 310 us -> 310 us  [both_factors(): factor = jnp.swapaxes(jnp.linalg.cholesky(gram_matrix), 1, 2)]
  transfers between devices with their start and end apart: 9 -> 16, of which waited for: 7 -> 9; matrix products, arithmetic and copies ran while one was open for 14% -> 15% of each run, Pallas kernels for 0% -> 0%
where the time goes in v1:
time: 1390 us; the launch traced here: 1380 us
  other arithmetic  994 us (72%)
  waiting for transfers between devices  179 us (13%)
  matrix products  94.6 us (7%)
  local copies, waits for them, and re-layouts  63.4 us (5%)
  starting transfers between devices  34.7 us (2%)
  between operations  14.6 us (1%)
    another operation x49, other arithmetic, merge_pair(): return jnp.swapaxes(jnp.linalg.cholesky(gram_matrix), 1, 2)  489 us
    another operation x17, other arithmetic, both_factors(): factor = jnp.swapaxes(jnp.linalg.cholesky(gram_matrix), 1, 2)  310 us
    another operation x16, other arithmetic, both_factors(): return jnp.swapaxes(jnp.linalg.cholesky(node_gram), 1, 2)  168 us
    ppermute x7, waiting for transfers between devices, partner(): return lax.ppermute(block, axis, route)  167 us
  transfers between devices with their start and end apart: 16, of which 9 were waited for; matrix products, arithmetic and copies ran while one was open for 15% of the time, Pallas kernels for 0%

profile of v1, /device:TPU:1, one launch (start us, length us, event | category | flops | bytes accessed | tf_op | source)
XLA Modules:
  0.0 1380.8 jit_solution(10003636659192546869)
XLA Ops:
  75.5 46.9 %custom-call.55 = f32[4,128,128]{2,1,0:T(8,128)S(1)} custom-call(f32[4,128,128]{2,1,0:T(8,128)S(1)} %cholesky.1016), custom_call_target="Cholesky" | custom-call | tf_op jit(solution)/shard_map/jit(cholesky)/cholesky | solution.py:42
  122.4 39.3 %custom-call.56 = f32[4,1,128,128]{2,3,1,0:T(8,128)S(1)} custom-call(f32[4,1,128,128]{3,2,1,0:T(8,128)S(1)} %select_bitcast_fusion.3), custom_call_target="InvertDiagBlocksLowerTriangular" | custom-call | tf_op jit(solution)/shard_map/jit(cholesky)/cholesky | solution.py:42
  170.2 48.2 %custom-call.57 = f32[4,128,128]{2,1,0:T(8,128)S(1)} custom-call(f32[4,128,128]{2,1,0:T(8,128)} %cholesky.1020), custom_call_target="Cholesky" | custom-call | tf_op jit(solution)/shard_map/jit(cholesky)/cholesky | solution.py:42
  220.1 39.3 %custom-call.58 = f32[4,1,128,128]{2,3,1,0:T(8,128)S(1)} custom-call(f32[4,1,128,128]{3,2,1,0:T(8,128)S(1)} %get-tuple-element.45), custom_call_target="InvertDiagBlocksLowerTriangular" | custom-call | tf_op jit(solution)/shard_map/jit(cholesky)/cholesky | solution.py:42
  263.6 46.9 %custom-call.59 = f32[4,128,128]{2,1,0:T(8,128)S(1)} custom-call(f32[4,128,128]{2,1,0:T(8,128)S(1)} %cholesky.1025), custom_call_target="Cholesky" | custom-call | tf_op jit(solution)/shard_map/jit(cholesky)/cholesky | solution.py:42
  311.3 39.5 %custom-call.60 = f32[4,1,128,128]{2,3,1,0:T(8,128)S(1)} custom-call(f32[4,1,128,128]{3,2,1,0:T(8,128)S(1)} %get-tuple-element.43), custom_call_target="InvertDiagBlocksLowerTriangular" | custom-call | tf_op jit(solution)/shard_map/jit(cholesky)/cholesky | solution.py:42
  354.5 46.9 %custom-call.61 = f32[4,128,128]{2,1,0:T(8,128)S(1)} custom-call(f32[4,128,128]{2,1,0:T(8,128)S(1)} %convolution_subtract_fusion.10), custom_call_target="Cholesky" | custom-call | tf_op jit(solution)/shard_map/jit(cholesky)/cholesky | solution.py:42
  428.7 23.5 %custom-call.83 = f32[2,128,128]{2,1,0:T(8,128)S(1)} custom-call(f32[2,128,128]{2,1,0:T(8,128)S(1)} %cholesky.1029), custom_call_target="Cholesky" | custom-call | tf_op jit(solution)/shard_map/jit(cholesky)/cholesky | solution.py:49
  478.7 25.3 %custom-call.85 = f32[2,128,128]{2,1,0:T(8,128)} custom-call(f32[2,128,128]{2,1,0:T(8,128)} %cholesky.1033), custom_call_target="Cholesky" | custom-call | tf_op jit(solution)/shard_map/jit(cholesky)/cholesky | solution.py:49
  531.0 24.9 %custom-call.87 = f32[2,128,128]{2,1,0:T(8,128)} custom-call(f32[2,128,128]{2,1,0:T(8,128)} %cholesky.1038), custom_call_target="Cholesky" | custom-call | tf_op jit(solution)/shard_map/jit(cholesky)/cholesky | solution.py:49
  582.1 25.1 %custom-call.89 = f32[2,128,128]{2,1,0:T(8,128)} custom-call(f32[2,128,128]{2,1,0:T(8,128)} %convolution_subtract_fusion.14), custom_call_target="Cholesky" | custom-call | tf_op jit(solution)/shard_map/jit(cholesky)/cholesky | solution.py:49
  664.4 23.9 %custom-call.90 = f32[2,128,128]{2,1,0:T(8,128)S(1)} custom-call(f32[2,128,128]{2,1,0:T(8,128)S(1)} %cholesky.1042), custom_call_target="Cholesky" | custom-call | tf_op jit(solution)/shard_map/jit(cholesky)/cholesky | solution.py:62
  714.7 24.9 %custom-call.92 = f32[2,128,128]{2,1,0:T(8,128)} custom-call(f32[2,128,128]{2,1,0:T(8,128)} %cholesky.1046), custom_call_target="Cholesky" | custom-call | tf_op jit(solution)/shard_map/jit(cholesky)/cholesky | solution.py:62
  766.8 24.9 %custom-call.94 = f32[2,128,128]{2,1,0:T(8,128)} custom-call(f32[2,128,128]{2,1,0:T(8,128)} %cholesky.1051), custom_call_target="Cholesky" | custom-call | tf_op jit(solution)/shard_map/jit(cholesky)/cholesky | solution.py:62
  817.7 25.1 %custom-call.96 = f32[2,128,128]{2,1,0:T(8,128)} custom-call(f32[2,128,128]{2,1,0:T(8,128)} %convolution_subtract_fusion.13), custom_call_target="Cholesky" | custom-call | tf_op jit(solution)/shard_map/jit(cholesky)/cholesky | solution.py:62
  911.4 23.9 %custom-call.97 = f32[2,128,128]{2,1,0:T(8,128)S(1)} custom-call(f32[2,128,128]{2,1,0:T(8,128)S(1)} %cholesky.1055), custom_call_target="Cholesky" | custom-call | tf_op jit(solution)/shard_map/jit(cholesky)/cholesky | solution.py:62
  961.7 24.9 %custom-call.99 = f32[2,128,128]{2,1,0:T(8,128)} custom-call(f32[2,128,128]{2,1,0:T(8,128)} %cholesky.1059), custom_call_target="Cholesky" | custom-call | tf_op jit(solution)/shard_map/jit(cholesky)/cholesky | solution.py:62
  1013.8 24.9 %custom-call.101 = f32[2,128,128]{2,1,0:T(8,128)} custom-call(f32[2,128,128]{2,1,0:T(8,128)} %cholesky.1064), custom_call_target="Cholesky" | custom-call | tf_op jit(solution)/shard_map/jit(cholesky)/cholesky | solution.py:62
  1064.8 25.1 %custom-call.103 = f32[2,128,128]{2,1,0:T(8,128)} custom-call(f32[2,128,128]{2,1,0:T(8,128)} %convolution_subtract_fusion.12), custom_call_target="Cholesky" | custom-call | tf_op jit(solution)/shard_map/jit(cholesky)/cholesky | solution.py:62
  1100.7 67.8 %collective-permute-done.11 = f32[512,512]{0,1:T(8,128)} collective-permute-done((f32[512,512]{0,1:T(8,128)}, f32[512,512]{0,1:T(8,128)}, u32[]{:S(2)}, u32[]{:S(2)}) %collective-permute-start.11) | collective-permute-done | bytes 1048608 | tf_op jit(solution)/shard_map/ppermute | solution.py:30
  1202.2 23.9 %custom-call.104 = f32[2,128,128]{2,1,0:T(8,128)S(1)} custom-call(f32[2,128,128]{2,1,0:T(8,128)S(1)} %cholesky.1068), custom_call_target="Cholesky" | custom-call | tf_op jit(solution)/shard_map/jit(cholesky)/cholesky | solution.py:62
  1250.4 23.5 %custom-call.106 = f32[2,128,128]{2,1,0:T(8,128)S(1)} custom-call(f32[2,128,128]{2,1,0:T(8,128)S(1)} %cholesky.1072), custom_call_target="Cholesky" | custom-call | tf_op jit(solution)/shard_map/jit(cholesky)/cholesky | solution.py:62
  1296.7 23.5 %custom-call.108 = f32[2,128,128]{2,1,0:T(8,128)S(1)} custom-call(f32[2,128,128]{2,1,0:T(8,128)S(1)} %cholesky.1077), custom_call_target="Cholesky" | custom-call | tf_op jit(solution)/shard_map/jit(cholesky)/cholesky | solution.py:62
  1341.7 23.7 %custom-call.110 = f32[2,128,128]{2,1,0:T(8,128)S(1)} custom-call(f32[2,128,128]{2,1,0:T(8,128)S(1)} %convolution_subtract_fusion.11), custom_call_target="Cholesky" | custom-call | tf_op jit(solution)/shard_map/jit(cholesky)/cholesky | solution.py:62
  (253 shorter events, 600.9 us)
Async XLA Ops:
  8.8 11.8 copy-start.22
  8.8 11.8 copy-start.23
  8.8 14.3 %collective-permute-start = (bf16[2,128,256]{2,1,0:T(8,128)(2,1)}, bf16[2,128,256]{2,1,0:T(8,128)(2,1)}, u32[]{:S(2)}, u32[]{:S(2)}) collective-permute-start(bf16[2,128,256]{2,1,0:T(8,128)(2,1)} %get-tuple-element.40), channel_id=1, source_target_pairs={{0,1},{1,0},{2,3},{3,2},{4,5},{5,4},{6,7},{7,6},{8,9},{9,8},{10,11... | collective-permute-start | bytes 393224 | tf_op jit(solution)/shard_map/ppermute | solution.py:74
  10.9 17.1 %collective-permute-start.1 = (bf16[2,128,256]{2,1,0:T(8,128)(2,1)}, bf16[2,128,256]{2,1,0:T(8,128)(2,1)}, u32[]{:S(2)}, u32[]{:S(2)}) collective-permute-start(bf16[2,128,256]{2,1,0:T(8,128)(2,1)} %get-tuple-element.39), channel_id=1, source_target_pairs={{0,2},{1,3},{2,0},{3,1},{4,6},{5,7},{6,4},{7,5},{8,10},{9,11},{10,... | collective-permute-start | bytes 393224 | tf_op jit(solution)/shard_map/ppermute | solution.py:74
  12.2 18.5 %collective-permute-start.2 = (bf16[2,128,256]{2,1,0:T(8,128)(2,1)}, bf16[2,128,256]{2,1,0:T(8,128)(2,1)}, u32[]{:S(2)}, u32[]{:S(2)}) collective-permute-start(bf16[2,128,256]{2,1,0:T(8,128)(2,1)} %get-tuple-element.38), channel_id=1, source_target_pairs={{0,3},{1,2},{2,1},{3,0},{4,7},{5,6},{6,5},{7,4},{8,11},{9,10},{10,... | collective-permute-start | bytes 393224 | tf_op jit(solution)/shard_map/ppermute | solution.py:74
  12.2 20.1 %collective-permute-start.3 = (bf16[2,128,256]{2,1,0:T(8,128)(2,1)}, bf16[2,128,256]{2,1,0:T(8,128)(2,1)}, u32[]{:S(2)}, u32[]{:S(2)}) collective-permute-start(bf16[2,128,256]{2,1,0:T(8,128)(2,1)} %get-tuple-element.37), channel_id=1, source_target_pairs={{0,4},{1,5},{2,6},{3,7},{4,0},{5,1},{6,2},{7,3},{8,12},{9,13},{10,... | collective-permute-start | bytes 393224 | tf_op jit(solution)/shard_map/ppermute | solution.py:74
  14.6 19.2 %collective-permute-start.4 = (bf16[2,128,256]{2,1,0:T(8,128)(2,1)}, bf16[2,128,256]{2,1,0:T(8,128)(2,1)}, u32[]{:S(2)}, u32[]{:S(2)}) collective-permute-start(bf16[2,128,256]{2,1,0:T(8,128)(2,1)} %get-tuple-element.36), channel_id=1, source_target_pairs={{0,5},{1,4},{2,7},{3,6},{4,1},{5,0},{6,3},{7,2},{8,13},{9,12},{10,... | collective-permute-start | bytes 393224 | tf_op jit(solution)/shard_map/ppermute | solution.py:74
  15.6 39.8 %all-to-all-start = ((bf16[16,128,256]{2,1,0:T(8,128)(2,1)}), bf16[16,128,256]{2,1,0:T(8,128)(2,1)}, u32[]{:S(2)}, u32[]{:S(2)}) async-start(bf16[16,128,256]{2,1,0:T(8,128)(2,1)} %param.12), calls=%async_computation | async-start | bytes 2097152 | tf_op jit(solution)/shard_map/all_to_all | solution.py:82
  20.2 1350.0 %all-gather.2.cloned.1.call-start = ((), (), s32[]{:S(2)}) async-start(), calls=%async_computation.1 | async-start | bytes 1179648 | tf_op jit(solution)/shard_map/all_gather | solution.py:106
  20.4 380.9 %copy-start.16 = (pred[128,128]{1,0:T(8,128)(4,1)}, pred[128,128]{1,0:T(8,128)(4,1)S(1)}, u32[]{:S(2)}) copy-start(pred[128,128]{1,0:T(8,128)(4,1)S(1)} %iota_compare_fusion.3) | copy-start | bytes 49156
  23.1 22.3 %collective-permute-start.5 = (bf16[2,128,256]{2,1,0:T(8,128)(2,1)}, bf16[2,128,256]{2,1,0:T(8,128)(2,1)S(1)}, u32[]{:S(2)}, u32[]{:S(2)}) collective-permute-start(bf16[2,128,256]{2,1,0:T(8,128)(2,1)} %get-tuple-element.35), channel_id=1, source_target_pairs={{0,6},{1,7},{2,4},{3,5},{4,2},{5,3},{6,0},{7,1},{8,14},{9,15},{10,... | collective-permute-start | bytes 393224 | tf_op jit(solution)/shard_map/ppermute | solution.py:74
  27.9 19.8 %collective-permute-start.6 = (bf16[2,128,256]{2,1,0:T(8,128)(2,1)}, bf16[2,128,256]{2,1,0:T(8,128)(2,1)S(1)}, u32[]{:S(2)}, u32[]{:S(2)}) collective-permute-start(bf16[2,128,256]{2,1,0:T(8,128)(2,1)} %get-tuple-element.34), channel_id=1, source_target_pairs={{0,7},{1,6},{2,5},{3,4},{4,3},{5,2},{6,1},{7,0},{8,15},{9,14},{10,... | collective-permute-start | bytes 393224 | tf_op jit(solution)/shard_map/ppermute | solution.py:74
  170.2 89.3 %copy-start.6 = (f32[4,384,128]{2,1,0:T(8,128)S(1)}, f32[4,384,128]{2,1,0:T(8,128)}, u32[]{:S(2)}) copy-start(f32[4,384,128]{2,1,0:T(8,128)} %copy-done.5) | copy-start | bytes 2359300
  609.8 3.0 copy-start.18
  610.0 23.0 %collective-permute-start.7 = (f32[512,512]{0,1:T(8,128)S(1)}, f32[512,512]{0,1:T(8,128)S(1)}, u32[]{:S(2)}, u32[]{:S(2)}) collective-permute-start(f32[512,512]{0,1:T(8,128)S(1)} %get-tuple-element.32), channel_id=1, source_target_pairs={{0,1},{1,0},{2,3},{3,2},{4,5},{5,4},{6,7},{7,6},{8,9},{9,8},{10,11... | collective-permute-start | bytes 3145736 | tf_op jit(solution)/shard_map/ppermute | solution.py:30
  611.0 44.5 %collective-permute-start.8 = (f32[512,512]{0,1:T(8,128)S(1)}, f32[512,512]{0,1:T(8,128)S(1)}, u32[]{:S(2)}, u32[]{:S(2)}) collective-permute-start(f32[512,512]{0,1:T(8,128)S(1)} %get-tuple-element.33), channel_id=1, source_target_pairs={{0,1},{1,0},{2,3},{3,2},{4,5},{5,4},{6,7},{7,6},{8,9},{9,8},{10,11... | collective-permute-start | bytes 3145736 | tf_op jit(solution)/shard_map/ppermute | solution.py:30
  845.5 14.8 %copy-start.20 = (f32[512]{0:T(512)S(1)}, f32[512]{0:T(512)}, u32[]{:S(2)}) copy-start(f32[512]{0:T(512)} %fusion.121) | copy-start | bytes 6148
  845.7 34.4 %collective-permute-start.9 = (f32[512,512]{0,1:T(8,128)S(1)}, f32[512,512]{0,1:T(8,128)S(1)}, u32[]{:S(2)}, u32[]{:S(2)}) collective-permute-start(f32[512,512]{0,1:T(8,128)S(1)} %get-tuple-element.30), channel_id=1, source_target_pairs={{0,2},{2,0},{1,3},{3,1},{4,6},{6,4},{5,7},{7,5},{8,10},{10,8},{9,1... | collective-permute-start | bytes 3145736 | tf_op jit(solution)/shard_map/ppermute | solution.py:30
  859.0 43.5 %collective-permute-start.10 = (f32[512,512]{0,1:T(8,128)S(1)}, f32[512,512]{0,1:T(8,128)S(1)}, u32[]{:S(2)}, u32[]{:S(2)}) collective-permute-start(f32[512,512]{0,1:T(8,128)S(1)} %get-tuple-element.31), channel_id=1, source_target_pairs={{0,2},{2,0},{1,3},{3,1},{4,6},{6,4},{5,7},{7,5},{8,10},{10,8},{9,1... | collective-permute-start | bytes 3145736 | tf_op jit(solution)/shard_map/ppermute | solution.py:30
  1092.5 3.9 copy-start.19
  1094.0 74.5 %collective-permute-start.11 = (f32[512,512]{0,1:T(8,128)}, f32[512,512]{0,1:T(8,128)}, u32[]{:S(2)}, u32[]{:S(2)}) collective-permute-start(f32[512,512]{0,1:T(8,128)} %get-tuple-element.28), channel_id=1, source_target_pairs={{0,4},{4,0},{1,5},{5,1},{2,6},{6,2},{3,7},{7,3},{8,12},{12,8},{9,1... | collective-permute-start | bytes 3145736 | tf_op jit(solution)/shard_map/ppermute | solution.py:30
  1096.0 95.0 %collective-permute-start.12 = (f32[512,512]{0,1:T(8,128)}, f32[512,512]{0,1:T(8,128)}, u32[]{:S(2)}, u32[]{:S(2)}) collective-permute-start(f32[512,512]{0,1:T(8,128)} %get-tuple-element.29), channel_id=1, source_target_pairs={{0,4},{4,0},{1,5},{5,1},{2,6},{6,2},{3,7},{7,3},{8,12},{12,8},{9,1... | collective-permute-start | bytes 3145736 | tf_op jit(solution)/shard_map/ppermute | solution.py:30
  1273.9 91.5 %copy-start.17 = (pred[128,128]{1,0:T(8,128)(4,1)S(1)}, pred[128,128]{1,0:T(8,128)(4,1)}, u32[]{:S(2)}) copy-start(pred[128,128]{1,0:T(8,128)(4,1)} %copy-done.16) | copy-start | bytes 49156
  1367.5 4.8 collective-permute-start.13
  (16 other events, 19.5 us)
Sparse Core Ops, SparseCore 0:
  1096.5 114.2 all-gather.1
